TPU v7x, 256 devices: a whole 4x4x8 slice. The times are simulated.
256 devices in a mesh: row: 64 (over x, z, core), col: 4 (over y).
Axes of the slice: x: 4, y: 4, z: 8, core: 2. Of those that a mesh axis runs over, the one named last changes fastest.
Arguments:
- factor: bfloat16 [64, 16, 4, 256, 256], P('row', None, 'col'), may hold values from -0.09375 to 0.09375
- diag_inverse: bfloat16 [64, 256, 256], P('row'), may hold values from -2 to 2, as said below
- right_side: bfloat16 [64, 64, 256], P('row'), may hold values from -6 to 6
- levels: int32 [64], replicated, may hold values from 0 to 3
- pattern: int32 [64, 16, 4], P('row', None, 'col'), may hold values 0 or 1
Outputs:
- forward: bfloat16 [64, 64, 256], P('row')
- solution: bfloat16 [64, 64, 256], P('row')
Inputs may be any that keep to these rules, and one draw needn't show every extreme that they name: `diag_inverse`: each block is the inverse of a factor diagonal block, nonsingular.
All inputs are finite; a program needn't handle non-finite values. No bound on the sum of `pattern` on one device may be relied on, other than what follows from the above.
Results may differ from a plain program's by a relative error of at most 0.014.
Values may be sent and summed in bfloat16 or wider, within the bound.
No kernel may reach another device: no remote copies, remote signals or barrier semaphores. Data moves between devices by JAX's collectives and lax.ppermute only.
A program may use at most 64 MiB of HBM per device.

v0:
```python
import jax
import jax.numpy as jnp
from jax import lax
from jax.sharding import PartitionSpec as P

LEVELS = 4


def shards(factor, diag_inverse, right_side, levels, pattern):
    col_blocks = factor.shape[1]
    width = factor.shape[3]
    n_cols = lax.axis_size("col")
    n_rhs = right_side.shape[1]
    row_index = lax.axis_index("row")
    col_index = lax.axis_index("col")
    blocks = factor.reshape(col_blocks, width, width)
    inverse = diag_inverse[0]
    own_level = lax.dynamic_index_in_dim(levels, row_index, 0, keepdims=False)
    col_levels = lax.dynamic_index_in_dim(
        levels.reshape(col_blocks, n_cols), col_index, 1, keepdims=False
    )
    usable = ((pattern.reshape(col_blocks) == 1) & (col_levels < own_level)).astype(jnp.bfloat16)
    usable_f = usable.astype(jnp.float32)
    solved = jnp.zeros((n_rhs, width), jnp.bfloat16)
    running = jnp.zeros((n_rhs, width), jnp.float32)
    for level in range(LEVELS):
        if level > 0:
            fresh_rows = jnp.where(own_level == level - 1, solved, jnp.zeros_like(solved))
            gathered = lax.all_gather(fresh_rows[None], "row", axis=0, tiled=True)
            classes = gathered.reshape(col_blocks, n_cols, n_rhs, width)
            mine = lax.dynamic_index_in_dim(classes, col_index, 1, keepdims=False)
            masked = mine * usable[:, None, None]
            running = running + jnp.einsum(
                "jkb,jab->ka", masked, blocks, preferred_element_type=jnp.float32
            )
            totals = lax.psum(running, "col")
        else:
            totals = running
        shifted = (right_side[0].astype(jnp.float32) - totals).astype(jnp.bfloat16)
        new_rows = jnp.einsum(
            "kb,ab->ka", shifted, inverse, preferred_element_type=jnp.float32
        ).astype(jnp.bfloat16)
        solved = jnp.where(own_level == level, new_rows, solved)
    result = jnp.zeros((n_rhs, width), jnp.bfloat16)
    backward_sum = jnp.zeros((n_rhs, width), jnp.float32)
    for level in range(LEVELS - 1, -1, -1):
        if level < LEVELS - 1:
            fresh_rows = jnp.where(own_level == level + 1, result, jnp.zeros_like(result))
            contrib = jnp.einsum(
                "ka,jab->jkb", fresh_rows, blocks, preferred_element_type=jnp.float32
            )
            contrib = contrib * usable_f[:, None, None]
            onehot = (jnp.arange(n_cols) == col_index).astype(jnp.float32)
            spread_out = (contrib[:, None] * onehot[None, :, None, None]).reshape(
                col_blocks * n_cols, n_rhs, width
            )
            summed = lax.psum_scatter(spread_out, "row", scatter_dimension=0, tiled=True)
            arrived = lax.psum(summed, "col")
            backward_sum = backward_sum + arrived[0]
        shifted = (solved.astype(jnp.float32) - backward_sum).astype(jnp.bfloat16)
        new_rows = jnp.einsum(
            "ka,ab->kb", shifted, inverse, preferred_element_type=jnp.float32
        ).astype(jnp.bfloat16)
        result = jnp.where(own_level == level, new_rows, result)
    return (solved[None], result[None])


def solution(mesh):
    return jax.shard_map(
        shards,
        mesh=mesh,
        in_specs=(
            P("row", None, "col", None, None),
            P("row", None, None),
            P("row", None, None),
            P(),
            P("row", None, "col"),
        ),
        out_specs=(P("row", None, None), P("row", None, None)),
        check_vma=False,
    )
```

profile of v0, /device:TPU:1, one launch (start us, length us, event | category | flops | bytes accessed | tf_op | source)
XLA Modules:
  0.0 986.6 jit_solution(4002698358978223013)
XLA Ops:
  7.3 1.4 dynamic_slice.18
  9.3 1.7 broadcast_select_fusion.2
  11.1 0.7 reshape.61
  11.8 0.8 fusion.96
  12.7 0.7 fusion.104
  13.3 79.5 %all-gather.7.cloned.1.call-done = bf16[4096,256]{1,0:T(8,128)(2,1)} async-done(((bf16[64,256]{1,0:T(8,128)(2,1)}), bf16[4096,256]{1,0:T(8,128)(2,1)}) %all-gather.7.cloned.1.call-update) | async-done | bytes 2097168 | tf_op jit(solution)/shard_map/all_gather | solution.py:29
  92.9 2.4 fusion.30
  96.0 40.8 %all-reduce.7.cloned.1.call-done = f32[64,256]{1,0:T(8,128)} async-done(((f32[64,256]{1,0:T(8,128)}), f32[64,256]{1,0:T(8,128)}) %all-reduce.7.cloned.1.call-update) | async-done | bytes 65552 | tf_op jit(solution)/shard_map/psum | solution.py:36
  136.8 1.6 broadcast_select_fusion.1
  138.5 82.1 %all-gather.9.cloned.1.call-done = bf16[4096,256]{1,0:T(8,128)(2,1)} async-done(((bf16[64,256]{1,0:T(8,128)(2,1)}), bf16[4096,256]{1,0:T(8,128)(2,1)}) %all-gather.9.cloned.1.call-update) | async-done | bytes 2097168 | tf_op jit(solution)/shard_map/all_gather | solution.py:29
  220.6 2.4 fusion.42
  223.7 40.7 %all-reduce.9.cloned.1.call-done = f32[64,256]{1,0:T(8,128)} async-done(((f32[64,256]{1,0:T(8,128)}), f32[64,256]{1,0:T(8,128)}) %all-reduce.9.cloned.1.call-update) | async-done | bytes 65552 | tf_op jit(solution)/shard_map/psum | solution.py:36
  264.5 1.6 broadcast_select_fusion
  266.8 80.9 %all-gather.11.cloned.1.call-done = bf16[4096,256]{1,0:T(8,128)(2,1)} async-done(((bf16[64,256]{1,0:T(8,128)(2,1)}), bf16[4096,256]{1,0:T(8,128)(2,1)}) %all-gather.11.cloned.1.call-update) | async-done | bytes 2097168 | tf_op jit(solution)/shard_map/all_gather | solution.py:29
  347.7 2.4 fusion.39
  350.3 41.3 %all-reduce.11.cloned.1.call-done = f32[64,256]{1,0:T(8,128)} async-done(((f32[64,256]{1,0:T(8,128)}), f32[64,256]{1,0:T(8,128)}) %all-reduce.11.cloned.1.call-update) | async-done | bytes 65552 | tf_op jit(solution)/shard_map/psum | solution.py:36
  391.6 1.0 fusion.48
  392.8 0.5 fusion.15
  393.3 2.3 bitcast_multiply_fusion.2
  395.7 141.5 %reduce-scatter.4.cloned.1.call-done = f32[1,64,256]{2,1,0:T(8,128)} async-done(((f32[64,64,256]{2,1,0:T(8,128)}), f32[1,64,256]{2,1,0:T(8,128)}) %reduce-scatter.4.cloned.1.call-update) | async-done | bytes 65552 | tf_op jit(solution)/shard_map/reduce_scatter | solution.py:57
  537.3 50.0 %all-reduce.13.cloned.1.call-done = f32[64,256]{1,0:T(8,128)} async-done(((f32[64,256]{1,0:T(8,128)}), f32[64,256]{1,0:T(8,128)}) %all-reduce.13.cloned.1.call-update) | async-done | bytes 65552 | tf_op jit(solution)/shard_map/psum | solution.py:58
  587.2 1.0 fusion.50
  588.2 0.5 fusion.21
  588.7 2.3 bitcast_multiply_fusion.1
  591.1 142.0 %reduce-scatter.6.cloned.1.call-done = f32[1,64,256]{2,1,0:T(8,128)} async-done(((f32[64,64,256]{2,1,0:T(8,128)}), f32[1,64,256]{2,1,0:T(8,128)}) %reduce-scatter.6.cloned.1.call-update) | async-done | bytes 65552 | tf_op jit(solution)/shard_map/reduce_scatter | solution.py:57
  733.2 49.5 %all-reduce.15.cloned.1.call-done = f32[64,256]{1,0:T(8,128)} async-done(((f32[64,256]{1,0:T(8,128)}), f32[64,256]{1,0:T(8,128)}) %all-reduce.15.cloned.1.call-update) | async-done | bytes 65552 | tf_op jit(solution)/shard_map/psum | solution.py:58
  782.7 0.8 add.46
  783.7 0.5 fusion.27
  784.2 2.3 bitcast_multiply_fusion
  786.6 142.0 %reduce-scatter.8.cloned.1.call-done = f32[1,64,256]{2,1,0:T(8,128)} async-done(((f32[64,64,256]{2,1,0:T(8,128)}), f32[1,64,256]{2,1,0:T(8,128)}) %reduce-scatter.8.cloned.1.call-update) | async-done | bytes 65552 | tf_op jit(solution)/shard_map/reduce_scatter | solution.py:57
  928.6 49.6 %all-reduce.17.cloned.1.call-done = f32[64,256]{1,0:T(8,128)} async-done(((f32[64,256]{1,0:T(8,128)}), f32[64,256]{1,0:T(8,128)}) %all-reduce.17.cloned.1.call-update) | async-done | bytes 65552 | tf_op jit(solution)/shard_map/psum | solution.py:58
  978.1 1.6 fusion.53
  (39 shorter events, 1.1 us)
Async XLA Ops:
  7.2 85.7 %copy-start = (bf16[1,16,1,256,256]{4,3,2,1,0:T(8,128)(2,1)S(1)}, bf16[1,16,1,256,256]{4,3,2,1,0:T(8,128)(2,1)}, u32[]{:S(2)}) copy-start(bf16[1,16,1,256,256]{4,3,2,1,0:T(8,128)(2,1)} %param.5) | copy-start | bytes 6291460
  7.2 129.6 %copy-start.1 = (bf16[1,256,256]{2,1,0:T(8,128)(2,1)S(1)}, bf16[1,256,256]{2,1,0:T(8,128)(2,1)}, u32[]{:S(2)}) copy-start(bf16[1,256,256]{2,1,0:T(8,128)(2,1)} %param.6) | copy-start | bytes 393220
  7.2 129.6 %copy-start.3 = (bf16[1,64,256]{2,1,0:T(8,128)(2,1)S(1)}, bf16[1,64,256]{2,1,0:T(8,128)(2,1)}, u32[]{:S(2)}) copy-start(bf16[1,64,256]{2,1,0:T(8,128)(2,1)} %param.7) | copy-start | bytes 98308
  7.2 85.6 %all-gather.7.cloned.1.call-start = ((), (), s32[]{:S(2)}) async-start(), calls=%async_computation.12 | async-start | bytes 2129920 | tf_op jit(solution)/shard_map/all_gather | solution.py:29
  11.0 125.7 %all-reduce.7.cloned.1.call-start = ((), (), s32[]{:S(2)}) async-start(), calls=%async_computation.3 | async-start | bytes 131072 | tf_op jit(solution)/shard_map/psum | solution.py:36
  95.3 125.3 %all-gather.9.cloned.1.call-start = ((), (), s32[]{:S(2)}) async-start(), calls=%async_computation.13 | async-start | bytes 2129920 | tf_op jit(solution)/shard_map/all_gather | solution.py:29
  138.4 126.0 %all-reduce.9.cloned.1.call-start = ((), (), s32[]{:S(2)}) async-start(), calls=%async_computation.4 | async-start | bytes 131072 | tf_op jit(solution)/shard_map/psum | solution.py:36
  223.0 124.7 %all-gather.11.cloned.1.call-start = ((), (), s32[]{:S(2)}) async-start(), calls=%async_computation.14 | async-start | bytes 2129920 | tf_op jit(solution)/shard_map/all_gather | solution.py:29
  266.1 125.5 %all-reduce.11.cloned.1.call-start = ((), (), s32[]{:S(2)}) async-start(), calls=%async_computation.5 | async-start | bytes 131072 | tf_op jit(solution)/shard_map/psum | solution.py:36
  350.2 187.0 %reduce-scatter.4.cloned.1.call-start = ((), (), s32[]{:S(2)}) async-start(), calls=%async_computation.6 | async-start | bytes 4259840 | tf_op jit(solution)/shard_map/reduce_scatter | solution.py:57
  392.6 585.5 %copy-start.2 = (bf16[64,256]{1,0:T(8,128)(2,1)}, bf16[64,256]{1,0:T(8,128)(2,1)S(1)}, u32[]{:S(2)}) copy-start(bf16[64,256]{1,0:T(8,128)(2,1)S(1)} %fusion.48) | copy-start | bytes 98308
  395.6 191.6 %all-reduce.13.cloned.1.call-start = ((), (), s32[]{:S(2)}) async-start(), calls=%async_computation.7 | async-start | bytes 131072 | tf_op jit(solution)/shard_map/psum | solution.py:58
  537.2 195.9 %reduce-scatter.6.cloned.1.call-start = ((), (), s32[]{:S(2)}) async-start(), calls=%async_computation.8 | async-start | bytes 4259840 | tf_op jit(solution)/shard_map/reduce_scatter | solution.py:57
  591.0 191.7 %copy-start.4 = (f32[64,256]{1,0:T(8,128)S(1)}, f32[64,256]{1,0:T(8,128)}, u32[]{:S(2)}) copy-start(f32[64,256]{1,0:T(8,128)} %all-reduce.13.cloned.1.call-done) | copy-start | bytes 196612
  591.0 191.6 %all-reduce.15.cloned.1.call-start = ((), (), s32[]{:S(2)}) async-start(), calls=%async_computation.9 | async-start | bytes 131072 | tf_op jit(solution)/shard_map/psum | solution.py:58
  733.1 195.4 %reduce-scatter.8.cloned.1.call-start = ((), (), s32[]{:S(2)}) async-start(), calls=%async_computation.10 | async-start | bytes 4259840 | tf_op jit(solution)/shard_map/reduce_scatter | solution.py:57
  786.5 191.6 %all-reduce.17.cloned.1.call-start = ((), (), s32[]{:S(2)}) async-start(), calls=%async_computation.11 | async-start | bytes 131072 | tf_op jit(solution)/shard_map/psum | solution.py:58
Sparse Core Ops, SparseCore 0:
  11.4 81.4 all-gather.6
  95.4 41.2 all-reduce.6
  140.5 80.0 all-gather.8
  223.1 41.2 all-reduce.8
  267.7 80.0 all-gather.10
  350.3 41.2 all-reduce.10
  396.3 140.8 reduce-scatter.3
  539.5 47.7 all-reduce.12
  591.9 141.1 reduce-scatter.5
  735.3 47.3 all-reduce.14
  787.4 141.1 reduce-scatter.7
  930.7 47.3 all-reduce.16
where the time goes:
time: 988 us; the launch traced here: 987 us
  waiting for transfers between devices  940 us (95%)
  matrix products  17.6 us (2%)
  between operations  16.9 us (2%)
    reduce_scatter x3, waiting for transfers between devices, shards(): lax.psum_scatter(spread_out, 'row', scatter_dimension=0, tiled=True)  426 us
    all_gather x3, waiting for transfers between devices, shards(): gathered = lax.all_gather(fresh_rows[None], 'row', axis=0, tiled=True)  243 us
    psum x3, waiting for transfers between devices, shards(): arrived = lax.psum(summed, 'col')  149 us
    psum x3, waiting for transfers between devices, shards(): totals = lax.psum(running, 'col')  123 us
  transfers between devices with their start and end apart: 12, of which 12 were waited for; matrix products, arithmetic and copies ran while one was open for 0% of the time, Pallas kernels for 0%

commit v1 on v0

v1 whole, which is shorter than its diff:
```python
import jax
import jax.numpy as jnp
from jax import lax
from jax.sharding import Mesh, PartitionSpec as P

LEVELS = 4
NX, NZ, NK, NY = 4, 8, 2, 4
HZ = NZ // 2


def cyclic(n, shift):
    return [(i, (i + shift) % n) for i in range(n)]


def swap(v):
    return lax.ppermute(v, "k", [(0, 1), (1, 0)])


def shards(factor, diag_inverse, right_side, levels, pattern):
    n_j, width = factor.shape[1], factor.shape[3]
    n_rhs = right_side.shape[1]
    half = n_rhs // NK
    x, z, k, y = (lax.axis_index(a) for a in ("x", "z", "k", "y"))
    z_even, odd = z % 2, y % 2
    own_row = (x * NZ + z) * NK + k
    l_own = factor.reshape(n_j, width, width)
    d_own = diag_inverse[0]
    b_all = right_side[0].reshape(NK, half, width)
    b_mine = lax.dynamic_index_in_dim(b_all, k, 0, keepdims=False)
    b_theirs = lax.dynamic_index_in_dim(b_all, 1 - k, 0, keepdims=False)
    level_own = lax.dynamic_index_in_dim(levels, own_row, 0, keepdims=False)
    level_par = lax.dynamic_index_in_dim(levels, own_row + 1 - 2 * k, 0, keepdims=False)
    col_levels = lax.dynamic_index_in_dim(levels.reshape(n_j, NY), y, 1, keepdims=False)
    u_own = ((pattern.reshape(n_j) == 1) & (col_levels < level_own)).astype(jnp.bfloat16)

    d_par = swap(d_own)
    b_par = swap(b_theirs)
    u_par = swap(u_own)
    l_par = swap(l_own)

    def solve(v, d):
        return jnp.einsum("kb,ab->ka", v, d, preferred_element_type=jnp.float32).astype(jnp.bfloat16)

    def solve_t(v, d):
        return jnp.einsum("ka,ab->kb", v, d, preferred_element_type=jnp.float32).astype(jnp.bfloat16)

    zero = jnp.zeros((half, width), jnp.bfloat16)
    f_own = jnp.where(level_own == 0, solve(b_mine, d_own), zero)
    f_par = jnp.where(level_par == 0, solve(b_par, d_par), zero)
    p_own = jnp.zeros((half, width), jnp.float32)
    p_par = jnp.zeros((half, width), jnp.float32)
    is_own = k == odd
    level_r = jnp.where(is_own, level_own, level_par)
    for level in range(1, LEVELS):
        f_r = jnp.where(is_own, f_own, f_par)
        sent = jnp.where(level_r == level - 1, f_r, zero)
        got = lax.all_to_all(jnp.broadcast_to(sent[None], (NZ, half, width)), "z", 0, 0)
        got = lax.dynamic_index_in_dim(got.reshape(HZ, 2, half, width), y // 2, 1, keepdims=False)
        parts = [lax.ppermute(got, "x", cyclic(NX, s)) for s in (3, 2, 1)] + [got]
        ring = jnp.concatenate(parts + parts[:-1], 0)
        cols = lax.dynamic_slice_in_dim(ring, (NX - 1 - x) * HZ, n_j, 0)
        p_own = p_own + jnp.einsum("jkb,jab->ka", cols * u_own[:, None, None], l_own, preferred_element_type=jnp.float32)
        p_par = p_par + jnp.einsum("jkb,jab->ka", cols * u_par[:, None, None], l_par, preferred_element_type=jnp.float32)
        rows = jnp.stack([jnp.where(k == 0, p_own, p_par), jnp.where(k == 0, p_par, p_own)]).astype(jnp.bfloat16)
        others = [lax.ppermute(rows, "y", cyclic(NY, s)).astype(jnp.float32) for s in (1, 2, 3)]
        other = others[0] + others[1] + others[2]
        s_own = p_own + jnp.where(k == 0, other[0], other[1])
        s_par = p_par + jnp.where(k == 0, other[1], other[0])
        f_own = jnp.where(level_own == level, solve((b_mine.astype(jnp.float32) - s_own).astype(jnp.bfloat16), d_own), f_own)
        f_par = jnp.where(level_par == level, solve((b_par.astype(jnp.float32) - s_par).astype(jnp.bfloat16), d_par), f_par)

    top = LEVELS - 1
    o_own = jnp.where(level_own == top, solve_t(f_own, d_own), zero)
    o_par = jnp.where(level_par == top, solve_t(f_par, d_par), zero)
    f_r = jnp.where(is_own, f_own, f_par)
    d_r = jnp.where(is_own, d_own, d_par)
    r_sum = jnp.zeros((half, width), jnp.float32)
    for level in range(top - 1, -1, -1):
        m_own = jnp.where(level_own == level + 1, o_own, zero)
        m_par = jnp.where(level_par == level + 1, o_par, zero)
        t = jnp.einsum("jka,jab->jkb", m_own[None] * u_own[:, None, None], l_own, preferred_element_type=jnp.float32)
        t = t + jnp.einsum("jka,jab->jkb", m_par[None] * u_par[:, None, None], l_par, preferred_element_type=jnp.float32)
        t = t.reshape(NX, HZ, half, width)
        mine = lax.dynamic_index_in_dim(t, x, 0, keepdims=False)
        for s in (1, 2, 3):
            piece = lax.dynamic_index_in_dim(t, (x + s) % NX, 0, keepdims=False).astype(jnp.bfloat16)
            mine = mine + lax.ppermute(piece, "x", cyclic(NX, s)).astype(jnp.float32)
        out = jnp.broadcast_to(mine.astype(jnp.bfloat16)[:, None], (HZ, 2, half, width)).reshape(NZ, half, width)
        arrived = lax.all_to_all(out, "z", 0, 0)
        r_sum = r_sum + jnp.sum(arrived.astype(jnp.float32), axis=0)
        o_r = solve_t((f_r.astype(jnp.float32) - r_sum).astype(jnp.bfloat16), d_r)
        got = jnp.stack([o_r] + [lax.ppermute(o_r, "y", cyclic(NY, s)) for s in (1, 2, 3)])
        new_own = lax.dynamic_index_in_dim(got, (y - 2 * z_even - k) % NY, 0, keepdims=False)
        new_par = lax.dynamic_index_in_dim(got, (y - 2 * z_even - 1 + k) % NY, 0, keepdims=False)
        o_own = jnp.where(level_own == level, new_own, o_own)
        o_par = jnp.where(level_par == level, new_par, o_par)

    theirs = swap(jnp.stack([f_par, o_par]))
    mine = jnp.stack([f_own, o_own])
    both = jnp.concatenate([jnp.where(k == 0, mine, theirs), jnp.where(k == 0, theirs, mine)], axis=1)
    return (both[0][None], both[1][None])


def solution(mesh):
    fine = Mesh(mesh.devices.reshape(NX, NZ, NK, NY), ("x", "z", "k", "y"))
    row = ("x", "z", "k")
    return jax.shard_map(
        shards,
        mesh=fine,
        in_specs=(
            P(row, None, "y", None, None),
            P(row, None, None),
            P(row, None, None),
            P(),
            P(row, None, "y"),
        ),
        out_specs=(P(row, None, None), P(row, None, None)),
        check_vma=False,
    )
```

time: 988 us -> 205 us (0.21)
  waiting for transfers between devices: 940 us -> 47.1 us
  starting transfers between devices: 0.49 us -> 79.4 us
  blocking collectives: 0 us -> 41.3 us
    reduce_scatter x3 -> x0, waiting for transfers between devices: 426 us -> none  [shards(): lax.psum_scatter(spread_out, 'row', scatter_dimension=0, tiled=True)]
    psum x6 -> x0, waiting for transfers between devices: 272 us -> none  [the longest x3 149 us: shards(): arrived = lax.psum(summed, 'col')]
    all_gather x3 -> x0, waiting for transfers between devices: 243 us -> none  [shards(): gathered = lax.all_gather(fresh_rows[None], 'row', axis=0, tiled=True)]
    ppermute x0 -> x41, starting transfers between devices: none -> 69.6 us  [the longest x5 28.6 us: swap(): return lax.ppermute(v, 'k', [(0, 1), (1, 0)])]
    all_to_all x0 -> x4, blocking collectives: none -> 41.3 us  [the longest x2 20.6 us: shards(): lax.all_to_all(jnp.broadcast_to(sent[None], (NZ, half, width)), 'z', 0, 0)]
    ppermute x0 -> x41, waiting for transfers between devices: none -> 32.4 us  [the longest x9 14.4 us: shards(): parts = [lax.ppermute(got, 'x', cyclic(NX, s)) for s in (3, 2, 1)] + [got]]
    all_to_all x0 -> x2, waiting for transfers between devices: none -> 14.7 us  [the longest x1 7.81 us: shards(): arrived = lax.all_to_all(out, 'z', 0, 0)]
    dot_general x14 -> x25, matrix products: 17.6 us -> 21.7 us  [the longest x3 7.11 us: shards(): jnp.einsum('jkb,jab->ka', cols * u_par[:, None, None], l_par, preferred_e...]
  transfers between devices with their start and end apart: 12 -> 43, of which waited for: 12 -> 30; matrix products, arithmetic and copies ran while one was open for 0% -> 4% of each run, Pallas kernels for 0% -> 0%
where the time goes in v1:
time: 205 us; the launch traced here: 204 us
  starting transfers between devices  79.4 us (39%)
  waiting for transfers between devices  47.1 us (23%)
  blocking collectives  41.3 us (20%)
  matrix products  21.7 us (11%)
  between operations  7.76 us (4%)
  local copies, waits for them, and re-layouts  4.5 us (2%)
  other arithmetic  2.5 us (1%)
    ppermute x5, starting transfers between devices, swap(): return lax.ppermute(v, 'k', [(0, 1), (1, 0)])  28.6 us
    all_to_all x2, blocking collectives, shards(): lax.all_to_all(jnp.broadcast_to(sent[None], (NZ, half, width)), 'z', 0, 0)  20.6 us
    all_to_all x2, blocking collectives, shards(): arrived = lax.all_to_all(out, 'z', 0, 0)  20.6 us
    ppermute x9, waiting for transfers between devices, shards(): parts = [lax.ppermute(got, 'x', cyclic(NX, s)) for s in (3, 2, 1)] + [got]  14.4 us
    ppermute x9, starting transfers between devices, shards(): lax.ppermute(rows, 'y', cyclic(NY, s)).astype(jnp.float32)  11.9 us
    ppermute x9, starting transfers between devices, shards(): lax.ppermute(o_r, 'y', cyclic(NY, s))  11.3 us
    ppermute x9, starting transfers between devices, shards(): mine = mine + lax.ppermute(piece, 'x', cyclic(NX, s)).astype(jnp.float32)  10.2 us
    ppermute x9, waiting for transfers between devices, shards(): mine = mine + lax.ppermute(piece, 'x', cyclic(NX, s)).astype(jnp.float32)  8.15 us
  transfers between devices with their start and end apart: 43, of which 30 were waited for; matrix products, arithmetic and copies ran while one was open for 4% of the time, Pallas kernels for 0%

profile of v1, /device:TPU:1, one launch (start us, length us, event | category | flops | bytes accessed | tf_op | source)
XLA Modules:
  0.0 204.2 jit_solution(736692178024066010)
XLA Ops:
  0.6 3.3 %collective-permute-start.1 = (bf16[256,256]{1,0:T(8,128)(2,1)}, bf16[256,256]{1,0:T(8,128)(2,1)S(1)}, u32[]{:S(2)}, u32[]{:S(2)}) collective-permute-start(bf16[256,256]{1,0:T(8,128)(2,1)} %bitcast.262), channel_id=1, source_target_pairs={{0,4},{4,0},{1,5},{5,1},{2,6},{6,2},{3,7},{7,3},{8,12},{12,8},{9,1... | collective-permute-start | bytes 393224 | tf_op jit(solution)/shard_map/ppermute | solution.py:16
  11.1 6.5 %all-to-all-start = ((bf16[8,32,256]{2,1,0:T(8,128)(2,1)}), bf16[8,32,256]{2,1,0:T(8,128)(2,1)S(1)}, u32[]{:S(2)}, u32[]{:S(2)}) async-start(bf16[8,32,256]{2,1,0:T(8,128)(2,1)} %broadcast_in_dim.15), calls=%async_computation | async-start | bytes 262144 | tf_op jit(solution)/shard_map/all_to_all | solution.py:57
  19.1 6.9 %all-to-all-done = bf16[8,32,256]{2,1,0:T(8,128)(2,1)S(1)} async-done(((bf16[8,32,256]{2,1,0:T(8,128)(2,1)}), bf16[8,32,256]{2,1,0:T(8,128)(2,1)S(1)}, u32[]{:S(2)}, u32[]{:S(2)}) %all-to-all-start) | async-done | bytes 131104 | tf_op jit(solution)/shard_map/all_to_all | solution.py:57
  26.0 2.5 %collective-permute-start.2 = (bf16[4,32,256]{2,1,0:T(8,128)(2,1)S(1)}, bf16[4,32,256]{2,1,0:T(8,128)(2,1)S(1)}, u32[]{:S(2)}, u32[]{:S(2)}) collective-permute-start(bf16[4,32,256]{2,1,0:T(8,128)(2,1)S(1)} %dynamic-slice_bitcast_fusion.2), channel_id=1, source_target_pairs={{0,192},{64,0},{128,64},{192,128},{1,193},{65,1},{129,65},{193,129... | collective-permute-start | bytes 196616 | tf_op jit(solution)/shard_map/ppermute | solution.py:59
  29.1 1.9 collective-permute-start.5
  32.1 4.1 %collective-permute-done.3 = bf16[4,32,256]{2,1,0:T(8,128)(2,1)S(1)} collective-permute-done((bf16[4,32,256]{2,1,0:T(8,128)(2,1)S(1)}, bf16[4,32,256]{2,1,0:T(8,128)(2,1)S(1)}, u32[]{:S(2)}, u32[]{:S(2)}) %collective-permute-start.3) | collective-permute-done | bytes 65568 | tf_op jit(solution)/shard_map/ppermute | solution.py:59
  36.2 1.7 collective-permute-done.4
  38.0 2.4 %convolution_bitcast_fusion.5 = f32[32,256]{1,0:T(8,128)S(1)} fusion(bf16[28,32,256]{2,1,0:T(8,128)(2,1)S(1)} %constant_dynamic-update-slice_fusion, s32[]{:T(128)S(6)} %select_n.373, bf16[16]{0:T(256)(128)(2,1)S(1)} %fusion.123, bf16[1,16,1,256,256]{4,3,2,1,0:T(8,128)(2,1)} %param.5), kind=kOutput, calls=%fused_computation.12 | convolution fusion | flops 67239936 | bytes 2392580 | tf_op jit(solution)/shard_map/jkb,jab->ka/dot_general | solution.py:62
  40.4 2.5 %convolution_bitcast_fusion.4 = f32[32,256]{1,0:T(8,128)S(1)} fusion(bf16[16,256,256]{2,1,0:T(8,128)(2,1)} %collective-permute-done.6, bf16[28,32,256]{2,1,0:T(8,128)(2,1)S(1)} %constant_dynamic-update-slice_fusion, s32[]{:T(128)S(6)} %select_n.373, bf16[16]{0:T(256)(128)(2,1)S(1)} %collective-permute-done.5), kind=kOutput, calls=%fused_computation.11 | convolution fusion | flops 67239936 | bytes 2392580 | tf_op jit(solution)/shard_map/jkb,jab->ka/dot_general | solution.py:63
  44.3 2.6 %collective-permute-start.8 = (bf16[2,32,256]{2,1,0:T(8,128)(2,1)S(1)}, bf16[2,32,256]{2,1,0:T(8,128)(2,1)S(1)}, u32[]{:S(2)}, u32[]{:S(2)}) collective-permute-start(bf16[2,32,256]{2,1,0:T(8,128)(2,1)S(1)} %pad_maximum_fusion.4), channel_id=1, source_target_pairs={{0,2},{1,3},{2,0},{3,1},{4,6},{5,7},{6,4},{7,5},{8,10},{9,11},{10,... | collective-permute-start | bytes 98312 | tf_op jit(solution)/shard_map/ppermute | solution.py:65
  50.4 10.3 %all_to_all.30 = bf16[8,32,256]{2,1,0:T(8,128)(2,1)S(1)} all-to-all(bf16[8,32,256]{2,1,0:T(8,128)(2,1)S(1)} %broadcast_in_dim.16), channel_id=1, replica_groups=mesh['x'=4,'z'=8,'k'=2,'y'=4] {'z'}, dimensions={0} | all-to-all | bytes 262144 | tf_op jit(solution)/shard_map/all_to_all | solution.py:57
  67.1 2.3 %fusion.2 = f32[32,256]{1,0:T(8,128)S(1)} fusion(f32[32,256]{1,0:T(8,128)S(1)} %convolution_bitcast_fusion.4, bf16[16,256,256]{2,1,0:T(8,128)(2,1)} %collective-permute-done.6, bf16[28,32,256]{2,1,0:T(8,128)(2,1)S(1)} %constant_dynamic-update-slice_fusion.7, s32[]{:T(128)S(6)} %select_n.373, bf16[16]{0:T(256)(128)(2,1)S(1)} %collective-permute-done.5), kind=kOutput, calls=%fused_computation.8 | convolution fusion | flops 67248128 | bytes 2425348 | tf_op jit(solution)/shard_map/jkb,jab->ka/dot_general | solution.py:63
  69.5 3.2 %collective-permute-start.14 = (bf16[2,32,256]{2,1,0:T(8,128)(2,1)S(1)}, bf16[2,32,256]{2,1,0:T(8,128)(2,1)S(1)}, u32[]{:S(2)}, u32[]{:S(2)}) collective-permute-start(bf16[2,32,256]{2,1,0:T(8,128)(2,1)S(1)} %pad_maximum_fusion.5), channel_id=1, source_target_pairs={{0,2},{1,3},{2,0},{3,1},{4,6},{5,7},{6,4},{7,5},{8,10},{9,11},{10,... | collective-permute-start | bytes 98312 | tf_op jit(solution)/shard_map/ppermute | solution.py:65
  75.9 10.3 %all_to_all.31 = bf16[8,32,256]{2,1,0:T(8,128)(2,1)S(1)} all-to-all(bf16[8,32,256]{2,1,0:T(8,128)(2,1)S(1)} %broadcast_in_dim.17), channel_id=1, replica_groups=mesh['x'=4,'z'=8,'k'=2,'y'=4] {'z'}, dimensions={0} | all-to-all | bytes 262144 | tf_op jit(solution)/shard_map/all_to_all | solution.py:57
  89.7 3.0 %collective-permute-done.17 = bf16[4,32,256]{2,1,0:T(8,128)(2,1)S(1)} collective-permute-done((bf16[4,32,256]{2,1,0:T(8,128)(2,1)S(1)}, bf16[4,32,256]{2,1,0:T(8,128)(2,1)S(1)}, u32[]{:S(2)}, u32[]{:S(2)}) %collective-permute-start.17) | collective-permute-done | bytes 65568 | tf_op jit(solution)/shard_map/ppermute | solution.py:59
  94.2 2.3 %fusion = f32[32,256]{1,0:T(8,128)S(1)} fusion(f32[32,256]{1,0:T(8,128)S(1)} %fusion.2, bf16[16,256,256]{2,1,0:T(8,128)(2,1)} %collective-permute-done.6, bf16[28,32,256]{2,1,0:T(8,128)(2,1)S(1)} %constant_dynamic-update-slice_fusion.14, s32[]{:T(128)S(6)} %select_n.373, bf16[16]{0:T(256)(128)(2,1)S(1)} %collective-permute-done.5), kind=kOutput, calls=%fused_computation.4 | convolution fusion | flops 67248128 | bytes 2425348 | tf_op jit(solution)/shard_map/jkb,jab->ka/dot_general | solution.py:63
  96.6 2.4 %collective-permute-start.20 = (bf16[2,32,256]{2,1,0:T(8,128)(2,1)S(1)}, bf16[2,32,256]{2,1,0:T(8,128)(2,1)S(1)}, u32[]{:S(2)}, u32[]{:S(2)}) collective-permute-start(bf16[2,32,256]{2,1,0:T(8,128)(2,1)S(1)} %pad_maximum_fusion.6), channel_id=1, source_target_pairs={{0,2},{1,3},{2,0},{3,1},{4,6},{5,7},{6,4},{7,5},{8,10},{9,11},{10,... | collective-permute-start | bytes 98312 | tf_op jit(solution)/shard_map/ppermute | solution.py:65
  103.1 2.1 %convolution_add_fusion.2 = f32[16,32,256]{2,1,0:T(8,128)S(1)} fusion(f32[16,32,256]{2,1,0:T(8,128)S(1)} %fusion.21, bf16[16,256,256]{2,1,0:T(8,128)(2,1)} %collective-permute-done.6, bf16[32,256]{1,0:T(8,128)(2,1)S(1)} %get-tuple-element.41, bf16[16]{0:T(256)(128)(2,1)S(1)} %collective-permute-done.5), kind=kOutput, calls=%fused_computation.2 | convolution fusion | flops 67371008 | bytes 3162144 | tf_op jit(solution)/shard_map/jka,jab->jkb/dot_general | solution.py:82
  108.4 2.2 %collective-permute-done.22 = bf16[4,32,256]{2,1,0:T(8,128)(2,1)S(1)} collective-permute-done((bf16[4,32,256]{2,1,0:T(8,128)(2,1)S(1)}, bf16[4,32,256]{2,1,0:T(8,128)(2,1)S(1)}, u32[]{:S(2)}, u32[]{:S(2)}) %collective-permute-start.22) | collective-permute-done | bytes 65568 | tf_op jit(solution)/shard_map/ppermute | solution.py:87
  111.6 3.4 %all-to-all-start.3 = ((bf16[8,32,256]{2,1,0:T(8,128)(2,1)}), bf16[8,32,256]{2,1,0:T(8,128)(2,1)S(1)}, u32[]{:S(2)}, u32[]{:S(2)}) async-start(bf16[8,32,256]{2,1,0:T(8,128)(2,1)} %bitcast.38), calls=%async_computation.3 | async-start | bytes 262144 | tf_op jit(solution)/shard_map/all_to_all | solution.py:89
  115.0 7.8 %all-to-all-done.3 = bf16[8,32,256]{2,1,0:T(8,128)(2,1)S(1)} async-done(((bf16[8,32,256]{2,1,0:T(8,128)(2,1)}), bf16[8,32,256]{2,1,0:T(8,128)(2,1)S(1)}, u32[]{:S(2)}, u32[]{:S(2)}) %all-to-all-start.3) | async-done | bytes 131104 | tf_op jit(solution)/shard_map/all_to_all | solution.py:89
  123.8 2.8 %collective-permute-start.26 = (bf16[32,256]{1,0:T(8,128)(2,1)S(1)}, bf16[32,256]{1,0:T(8,128)(2,1)S(1)}, u32[]{:S(2)}, u32[]{:S(2)}) collective-permute-start(bf16[32,256]{1,0:T(8,128)(2,1)S(1)} %convolution_convert_fusion.2), channel_id=1, source_target_pairs={{0,2},{1,3},{2,0},{3,1},{4,6},{5,7},{6,4},{7,5},{8,10},{9,11},{10,... | collective-permute-start | bytes 49160 | tf_op jit(solution)/shard_map/ppermute | solution.py:92
  129.7 2.1 %convolution_add_fusion.1 = f32[16,32,256]{2,1,0:T(8,128)S(1)} fusion(f32[16,32,256]{2,1,0:T(8,128)S(1)} %fusion.18, bf16[16,256,256]{2,1,0:T(8,128)(2,1)} %collective-permute-done.6, bf16[32,256]{1,0:T(8,128)(2,1)S(1)} %get-tuple-element.23, bf16[16]{0:T(256)(128)(2,1)S(1)} %collective-permute-done.5), kind=kOutput, calls=%fused_computation.1 | convolution fusion | flops 67371008 | bytes 3162144 | tf_op jit(solution)/shard_map/jka,jab->jkb/dot_general | solution.py:82
  132.6 2.8 %collective-permute-start.29 = (bf16[4,32,256]{2,1,0:T(8,128)(2,1)S(1)}, bf16[4,32,256]{2,1,0:T(8,128)(2,1)S(1)}, u32[]{:S(2)}, u32[]{:S(2)}) collective-permute-start(bf16[4,32,256]{2,1,0:T(8,128)(2,1)S(1)} %get-tuple-element.11), channel_id=1, source_target_pairs={{0,128},{64,192},{128,0},{192,64},{1,129},{65,193},{129,1},{193,65... | collective-permute-start | bytes 196616 | tf_op jit(solution)/shard_map/ppermute | solution.py:87
  138.6 10.3 %all_to_all.32 = bf16[8,32,256]{2,1,0:T(8,128)(2,1)S(1)} all-to-all(bf16[8,32,256]{2,1,0:T(8,128)(2,1)S(1)} %bitcast.275), channel_id=1, replica_groups=mesh['x'=4,'z'=8,'k'=2,'y'=4] {'z'}, dimensions={0} | all-to-all | bytes 262144 | tf_op jit(solution)/shard_map/all_to_all | solution.py:89
  149.1 2.6 %collective-permute-start.32 = (bf16[32,256]{1,0:T(8,128)(2,1)S(1)}, bf16[32,256]{1,0:T(8,128)(2,1)S(1)}, u32[]{:S(2)}, u32[]{:S(2)}) collective-permute-start(bf16[32,256]{1,0:T(8,128)(2,1)S(1)} %convolution_convert_fusion.1), channel_id=1, source_target_pairs={{0,2},{1,3},{2,0},{3,1},{4,6},{5,7},{6,4},{7,5},{8,10},{9,11},{10,... | collective-permute-start | bytes 49160 | tf_op jit(solution)/shard_map/ppermute | solution.py:92
  155.1 2.1 %convolution_add_fusion = f32[16,32,256]{2,1,0:T(8,128)S(1)} fusion(f32[16,32,256]{2,1,0:T(8,128)S(1)} %fusion.15, bf16[16,256,256]{2,1,0:T(8,128)(2,1)} %collective-permute-done.6, bf16[32,256]{1,0:T(8,128)(2,1)S(1)} %get-tuple-element.15, bf16[16]{0:T(256)(128)(2,1)S(1)} %collective-permute-done.5), kind=kOutput, calls=%fused_computation | convolution fusion | flops 67371008 | bytes 3162144 | tf_op jit(solution)/shard_map/jka,jab->jkb/dot_general | solution.py:82
  157.4 2.5 %collective-permute-start.35 = (bf16[4,32,256]{2,1,0:T(8,128)(2,1)S(1)}, bf16[4,32,256]{2,1,0:T(8,128)(2,1)S(1)}, u32[]{:S(2)}, u32[]{:S(2)}) collective-permute-start(bf16[4,32,256]{2,1,0:T(8,128)(2,1)S(1)} %get-tuple-element.8), channel_id=1, source_target_pairs={{0,128},{64,192},{128,0},{192,64},{1,129},{65,193},{129,1},{193,65... | collective-permute-start | bytes 196616 | tf_op jit(solution)/shard_map/ppermute | solution.py:87
  160.7 1.9 collective-permute-done.34
  163.3 10.3 %all_to_all.33 = bf16[8,32,256]{2,1,0:T(8,128)(2,1)S(1)} all-to-all(bf16[8,32,256]{2,1,0:T(8,128)(2,1)S(1)} %bitcast.276), channel_id=1, replica_groups=mesh['x'=4,'z'=8,'k'=2,'y'=4] {'z'}, dimensions={0} | all-to-all | bytes 262144 | tf_op jit(solution)/shard_map/all_to_all | solution.py:89
  174.4 2.8 %collective-permute-start.38 = (bf16[32,256]{1,0:T(8,128)(2,1)S(1)}, bf16[32,256]{1,0:T(8,128)(2,1)S(1)}, u32[]{:S(2)}, u32[]{:S(2)}) collective-permute-start(bf16[32,256]{1,0:T(8,128)(2,1)S(1)} %convolution_convert_fusion), channel_id=1, source_target_pairs={{0,2},{1,3},{2,0},{3,1},{4,6},{5,7},{6,4},{7,5},{8,10},{9,11},{10,... | collective-permute-start | bytes 49160 | tf_op jit(solution)/shard_map/ppermute | solution.py:92
  179.8 22.9 %collective-permute-start.40 = (bf16[2,32,256]{2,1,0:T(8,128)(2,1)S(1)}, bf16[2,32,256]{2,1,0:T(8,128)(2,1)S(1)}, u32[]{:S(2)}, u32[]{:S(2)}) collective-permute-start(bf16[2,32,256]{2,1,0:T(8,128)(2,1)S(1)} %pad_maximum_fusion.8), channel_id=1, source_target_pairs={{0,4},{4,0},{1,5},{5,1},{2,6},{6,2},{3,7},{7,3},{8,12},{12,8},{9,1... | collective-permute-start | bytes 98312 | tf_op jit(solution)/shard_map/ppermute | solution.py:16
  (153 shorter events, 49.7 us)
Async XLA Ops:
  0.6 8.5 %collective-permute-start.1 = (bf16[256,256]{1,0:T(8,128)(2,1)}, bf16[256,256]{1,0:T(8,128)(2,1)S(1)}, u32[]{:S(2)}, u32[]{:S(2)}) collective-permute-start(bf16[256,256]{1,0:T(8,128)(2,1)} %bitcast.262), channel_id=1, source_target_pairs={{0,4},{4,0},{1,5},{5,1},{2,6},{6,2},{3,7},{7,3},{8,12},{12,8},{9,1... | collective-permute-start | bytes 393224 | tf_op jit(solution)/shard_map/ppermute | solution.py:16
  4.0 36.5 %collective-permute-start.6 = (bf16[16,256,256]{2,1,0:T(8,128)(2,1)}, bf16[16,256,256]{2,1,0:T(8,128)(2,1)}, u32[]{:S(2)}, u32[]{:S(2)}) collective-permute-start(bf16[16,256,256]{2,1,0:T(8,128)(2,1)} %bitcast.261), channel_id=1, source_target_pairs={{0,4},{4,0},{1,5},{5,1},{2,6},{6,2},{3,7},{7,3},{8,12},{12,8},{9,1... | collective-permute-start | bytes 6291464 | tf_op jit(solution)/shard_map/ppermute | solution.py:16
  4.8 4.3 %collective-permute-start = (bf16[32,256]{1,0:T(8,128)(2,1)S(1)}, bf16[32,256]{1,0:T(8,128)(2,1)S(1)}, u32[]{:S(2)}, u32[]{:S(2)}) collective-permute-start(bf16[32,256]{1,0:T(8,128)(2,1)S(1)} %dynamic-slice_bitcast_fusion.3), channel_id=1, source_target_pairs={{0,4},{4,0},{1,5},{5,1},{2,6},{6,2},{3,7},{7,3},{8,12},{12,8},{9,1... | collective-permute-start | bytes 49160 | tf_op jit(solution)/shard_map/ppermute | solution.py:16
  11.1 14.9 %all-to-all-start = ((bf16[8,32,256]{2,1,0:T(8,128)(2,1)}), bf16[8,32,256]{2,1,0:T(8,128)(2,1)S(1)}, u32[]{:S(2)}, u32[]{:S(2)}) async-start(bf16[8,32,256]{2,1,0:T(8,128)(2,1)} %broadcast_in_dim.15), calls=%async_computation | async-start | bytes 262144 | tf_op jit(solution)/shard_map/all_to_all | solution.py:57
  26.0 6.1 %collective-permute-start.2 = (bf16[4,32,256]{2,1,0:T(8,128)(2,1)S(1)}, bf16[4,32,256]{2,1,0:T(8,128)(2,1)S(1)}, u32[]{:S(2)}, u32[]{:S(2)}) collective-permute-start(bf16[4,32,256]{2,1,0:T(8,128)(2,1)S(1)} %dynamic-slice_bitcast_fusion.2), channel_id=1, source_target_pairs={{0,192},{64,0},{128,64},{192,128},{1,193},{65,1},{129,65},{193,129... | collective-permute-start | bytes 196616 | tf_op jit(solution)/shard_map/ppermute | solution.py:59
  29.1 11.3 %collective-permute-start.5 = (bf16[16]{0:T(256)(128)(2,1)S(1)}, bf16[16]{0:T(256)(128)(2,1)S(1)}, u32[]{:S(2)}, u32[]{:S(2)}) collective-permute-start(bf16[16]{0:T(256)(128)(2,1)S(1)} %fusion.123), channel_id=1, source_target_pairs={{0,4},{4,0},{1,5},{5,1},{2,6},{6,2},{3,7},{7,3},{8,12},{12,8},{9,1... | collective-permute-start | bytes 104 | tf_op jit(solution)/shard_map/ppermute | solution.py:16
  31.0 5.2 %collective-permute-start.3 = (bf16[4,32,256]{2,1,0:T(8,128)(2,1)S(1)}, bf16[4,32,256]{2,1,0:T(8,128)(2,1)S(1)}, u32[]{:S(2)}, u32[]{:S(2)}) collective-permute-start(bf16[4,32,256]{2,1,0:T(8,128)(2,1)S(1)} %dynamic-slice_bitcast_fusion.2), channel_id=1, source_target_pairs={{0,128},{64,192},{128,0},{192,64},{1,129},{65,193},{129,1},{193,65... | collective-permute-start | bytes 196616 | tf_op jit(solution)/shard_map/ppermute | solution.py:59
  31.5 6.4 %collective-permute-start.4 = (bf16[4,32,256]{2,1,0:T(8,128)(2,1)S(1)}, bf16[4,32,256]{2,1,0:T(8,128)(2,1)S(1)}, u32[]{:S(2)}, u32[]{:S(2)}) collective-permute-start(bf16[4,32,256]{2,1,0:T(8,128)(2,1)S(1)} %dynamic-slice_bitcast_fusion.2), channel_id=1, source_target_pairs={{0,64},{64,128},{128,192},{192,0},{1,65},{65,129},{129,193},{193,1... | collective-permute-start | bytes 196616 | tf_op jit(solution)/shard_map/ppermute | solution.py:59
  42.9 6.4 %collective-permute-start.7 = (bf16[2,32,256]{2,1,0:T(8,128)(2,1)S(1)}, bf16[2,32,256]{2,1,0:T(8,128)(2,1)S(1)}, u32[]{:S(2)}, u32[]{:S(2)}) collective-permute-start(bf16[2,32,256]{2,1,0:T(8,128)(2,1)S(1)} %pad_maximum_fusion.4), channel_id=1, source_target_pairs={{0,1},{1,2},{2,3},{3,0},{4,5},{5,6},{6,7},{7,4},{8,9},{9,10},{10,1... | collective-permute-start | bytes 98312 | tf_op jit(solution)/shard_map/ppermute | solution.py:65
  44.3 5.0 %collective-permute-start.8 = (bf16[2,32,256]{2,1,0:T(8,128)(2,1)S(1)}, bf16[2,32,256]{2,1,0:T(8,128)(2,1)S(1)}, u32[]{:S(2)}, u32[]{:S(2)}) collective-permute-start(bf16[2,32,256]{2,1,0:T(8,128)(2,1)S(1)} %pad_maximum_fusion.4), channel_id=1, source_target_pairs={{0,2},{1,3},{2,0},{3,1},{4,6},{5,7},{6,4},{7,5},{8,10},{9,11},{10,... | collective-permute-start | bytes 98312 | tf_op jit(solution)/shard_map/ppermute | solution.py:65
  60.8 4.7 %collective-permute-start.11 = (bf16[4,32,256]{2,1,0:T(8,128)(2,1)S(1)}, bf16[4,32,256]{2,1,0:T(8,128)(2,1)S(1)}, u32[]{:S(2)}, u32[]{:S(2)}) collective-permute-start(bf16[4,32,256]{2,1,0:T(8,128)(2,1)S(1)} %dynamic-slice_bitcast_fusion.1), channel_id=1, source_target_pairs={{0,128},{64,192},{128,0},{192,64},{1,129},{65,193},{129,1},{193,65... | collective-permute-start | bytes 196616 | tf_op jit(solution)/shard_map/ppermute | solution.py:59
  61.3 4.9 %collective-permute-start.12 = (bf16[4,32,256]{2,1,0:T(8,128)(2,1)S(1)}, bf16[4,32,256]{2,1,0:T(8,128)(2,1)S(1)}, u32[]{:S(2)}, u32[]{:S(2)}) collective-permute-start(bf16[4,32,256]{2,1,0:T(8,128)(2,1)S(1)} %dynamic-slice_bitcast_fusion.1), channel_id=1, source_target_pairs={{0,64},{64,128},{128,192},{192,0},{1,65},{65,129},{129,193},{193,1... | collective-permute-start | bytes 196616 | tf_op jit(solution)/shard_map/ppermute | solution.py:59
  69.4 4.7 %collective-permute-start.13 = (bf16[2,32,256]{2,1,0:T(8,128)(2,1)S(1)}, bf16[2,32,256]{2,1,0:T(8,128)(2,1)S(1)}, u32[]{:S(2)}, u32[]{:S(2)}) collective-permute-start(bf16[2,32,256]{2,1,0:T(8,128)(2,1)S(1)} %pad_maximum_fusion.5), channel_id=1, source_target_pairs={{0,1},{1,2},{2,3},{3,0},{4,5},{5,6},{6,7},{7,4},{8,9},{9,10},{10,1... | collective-permute-start | bytes 98312 | tf_op jit(solution)/shard_map/ppermute | solution.py:65
  69.5 4.9 %collective-permute-start.14 = (bf16[2,32,256]{2,1,0:T(8,128)(2,1)S(1)}, bf16[2,32,256]{2,1,0:T(8,128)(2,1)S(1)}, u32[]{:S(2)}, u32[]{:S(2)}) collective-permute-start(bf16[2,32,256]{2,1,0:T(8,128)(2,1)S(1)} %pad_maximum_fusion.5), channel_id=1, source_target_pairs={{0,2},{1,3},{2,0},{3,1},{4,6},{5,7},{6,4},{7,5},{8,10},{9,11},{10,... | collective-permute-start | bytes 98312 | tf_op jit(solution)/shard_map/ppermute | solution.py:65
  87.7 4.9 %collective-permute-start.17 = (bf16[4,32,256]{2,1,0:T(8,128)(2,1)S(1)}, bf16[4,32,256]{2,1,0:T(8,128)(2,1)S(1)}, u32[]{:S(2)}, u32[]{:S(2)}) collective-permute-start(bf16[4,32,256]{2,1,0:T(8,128)(2,1)S(1)} %dynamic-slice_bitcast_fusion), channel_id=1, source_target_pairs={{0,128},{64,192},{128,0},{192,64},{1,129},{65,193},{129,1},{193,65... | collective-permute-start | bytes 196616 | tf_op jit(solution)/shard_map/ppermute | solution.py:59
  88.8 4.6 %collective-permute-start.18 = (bf16[4,32,256]{2,1,0:T(8,128)(2,1)S(1)}, bf16[4,32,256]{2,1,0:T(8,128)(2,1)S(1)}, u32[]{:S(2)}, u32[]{:S(2)}) collective-permute-start(bf16[4,32,256]{2,1,0:T(8,128)(2,1)S(1)} %dynamic-slice_bitcast_fusion), channel_id=1, source_target_pairs={{0,64},{64,128},{128,192},{192,0},{1,65},{65,129},{129,193},{193,1... | collective-permute-start | bytes 196616 | tf_op jit(solution)/shard_map/ppermute | solution.py:59
  96.5 4.8 %collective-permute-start.19 = (bf16[2,32,256]{2,1,0:T(8,128)(2,1)S(1)}, bf16[2,32,256]{2,1,0:T(8,128)(2,1)S(1)}, u32[]{:S(2)}, u32[]{:S(2)}) collective-permute-start(bf16[2,32,256]{2,1,0:T(8,128)(2,1)S(1)} %pad_maximum_fusion.6), channel_id=1, source_target_pairs={{0,1},{1,2},{2,3},{3,0},{4,5},{5,6},{6,7},{7,4},{8,9},{9,10},{10,1... | collective-permute-start | bytes 98312 | tf_op jit(solution)/shard_map/ppermute | solution.py:65
  96.6 4.7 %collective-permute-start.20 = (bf16[2,32,256]{2,1,0:T(8,128)(2,1)S(1)}, bf16[2,32,256]{2,1,0:T(8,128)(2,1)S(1)}, u32[]{:S(2)}, u32[]{:S(2)}) collective-permute-start(bf16[2,32,256]{2,1,0:T(8,128)(2,1)S(1)} %pad_maximum_fusion.6), channel_id=1, source_target_pairs={{0,2},{1,3},{2,0},{3,1},{4,6},{5,7},{6,4},{7,5},{8,10},{9,11},{10,... | collective-permute-start | bytes 98312 | tf_op jit(solution)/shard_map/ppermute | solution.py:65
  105.2 5.4 %collective-permute-start.22 = (bf16[4,32,256]{2,1,0:T(8,128)(2,1)S(1)}, bf16[4,32,256]{2,1,0:T(8,128)(2,1)S(1)}, u32[]{:S(2)}, u32[]{:S(2)}) collective-permute-start(bf16[4,32,256]{2,1,0:T(8,128)(2,1)S(1)} %get-tuple-element.12), channel_id=1, source_target_pairs={{0,64},{64,128},{128,192},{192,0},{1,65},{65,129},{129,193},{193,1... | collective-permute-start | bytes 196616 | tf_op jit(solution)/shard_map/ppermute | solution.py:87
  105.3 5.3 %collective-permute-start.23 = (bf16[4,32,256]{2,1,0:T(8,128)(2,1)S(1)}, bf16[4,32,256]{2,1,0:T(8,128)(2,1)S(1)}, u32[]{:S(2)}, u32[]{:S(2)}) collective-permute-start(bf16[4,32,256]{2,1,0:T(8,128)(2,1)S(1)} %get-tuple-element.14), channel_id=1, source_target_pairs={{0,128},{64,192},{128,0},{192,64},{1,129},{65,193},{129,1},{193,65... | collective-permute-start | bytes 196616 | tf_op jit(solution)/shard_map/ppermute | solution.py:87
  106.8 4.1 %collective-permute-start.24 = (bf16[4,32,256]{2,1,0:T(8,128)(2,1)S(1)}, bf16[4,32,256]{2,1,0:T(8,128)(2,1)S(1)}, u32[]{:S(2)}, u32[]{:S(2)}) collective-permute-start(bf16[4,32,256]{2,1,0:T(8,128)(2,1)S(1)} %get-tuple-element.13), channel_id=1, source_target_pairs={{0,192},{64,0},{128,64},{192,128},{1,193},{65,1},{129,65},{193,129... | collective-permute-start | bytes 196616 | tf_op jit(solution)/shard_map/ppermute | solution.py:87
  111.6 11.2 %all-to-all-start.3 = ((bf16[8,32,256]{2,1,0:T(8,128)(2,1)}), bf16[8,32,256]{2,1,0:T(8,128)(2,1)S(1)}, u32[]{:S(2)}, u32[]{:S(2)}) async-start(bf16[8,32,256]{2,1,0:T(8,128)(2,1)} %bitcast.38), calls=%async_computation.3 | async-start | bytes 262144 | tf_op jit(solution)/shard_map/all_to_all | solution.py:89
  123.0 3.8 %collective-permute-start.25 = (bf16[32,256]{1,0:T(8,128)(2,1)S(1)}, bf16[32,256]{1,0:T(8,128)(2,1)S(1)}, u32[]{:S(2)}, u32[]{:S(2)}) collective-permute-start(bf16[32,256]{1,0:T(8,128)(2,1)S(1)} %convolution_convert_fusion.2), channel_id=1, source_target_pairs={{0,1},{1,2},{2,3},{3,0},{4,5},{5,6},{6,7},{7,4},{8,9},{9,10},{10,1... | collective-permute-start | bytes 49160 | tf_op jit(solution)/shard_map/ppermute | solution.py:92
  123.8 4.1 %collective-permute-start.26 = (bf16[32,256]{1,0:T(8,128)(2,1)S(1)}, bf16[32,256]{1,0:T(8,128)(2,1)S(1)}, u32[]{:S(2)}, u32[]{:S(2)}) collective-permute-start(bf16[32,256]{1,0:T(8,128)(2,1)S(1)} %convolution_convert_fusion.2), channel_id=1, source_target_pairs={{0,2},{1,3},{2,0},{3,1},{4,6},{5,7},{6,4},{7,5},{8,10},{9,11},{10,... | collective-permute-start | bytes 49160 | tf_op jit(solution)/shard_map/ppermute | solution.py:92
  131.8 4.6 %collective-permute-start.28 = (bf16[4,32,256]{2,1,0:T(8,128)(2,1)S(1)}, bf16[4,32,256]{2,1,0:T(8,128)(2,1)S(1)}, u32[]{:S(2)}, u32[]{:S(2)}) collective-permute-start(bf16[4,32,256]{2,1,0:T(8,128)(2,1)S(1)} %get-tuple-element.9), channel_id=1, source_target_pairs={{0,64},{64,128},{128,192},{192,0},{1,65},{65,129},{129,193},{193,1... | collective-permute-start | bytes 196616 | tf_op jit(solution)/shard_map/ppermute | solution.py:87
  132.6 5.2 %collective-permute-start.29 = (bf16[4,32,256]{2,1,0:T(8,128)(2,1)S(1)}, bf16[4,32,256]{2,1,0:T(8,128)(2,1)S(1)}, u32[]{:S(2)}, u32[]{:S(2)}) collective-permute-start(bf16[4,32,256]{2,1,0:T(8,128)(2,1)S(1)} %get-tuple-element.11), channel_id=1, source_target_pairs={{0,128},{64,192},{128,0},{192,64},{1,129},{65,193},{129,1},{193,65... | collective-permute-start | bytes 196616 | tf_op jit(solution)/shard_map/ppermute | solution.py:87
  149.1 4.1 %collective-permute-start.31 = (bf16[32,256]{1,0:T(8,128)(2,1)S(1)}, bf16[32,256]{1,0:T(8,128)(2,1)S(1)}, u32[]{:S(2)}, u32[]{:S(2)}) collective-permute-start(bf16[32,256]{1,0:T(8,128)(2,1)S(1)} %convolution_convert_fusion.1), channel_id=1, source_target_pairs={{0,1},{1,2},{2,3},{3,0},{4,5},{5,6},{6,7},{7,4},{8,9},{9,10},{10,1... | collective-permute-start | bytes 49160 | tf_op jit(solution)/shard_map/ppermute | solution.py:92
  149.1 4.3 %collective-permute-start.32 = (bf16[32,256]{1,0:T(8,128)(2,1)S(1)}, bf16[32,256]{1,0:T(8,128)(2,1)S(1)}, u32[]{:S(2)}, u32[]{:S(2)}) collective-permute-start(bf16[32,256]{1,0:T(8,128)(2,1)S(1)} %convolution_convert_fusion.1), channel_id=1, source_target_pairs={{0,2},{1,3},{2,0},{3,1},{4,6},{5,7},{6,4},{7,5},{8,10},{9,11},{10,... | collective-permute-start | bytes 49160 | tf_op jit(solution)/shard_map/ppermute | solution.py:92
  157.3 5.3 %collective-permute-start.34 = (bf16[4,32,256]{2,1,0:T(8,128)(2,1)S(1)}, bf16[4,32,256]{2,1,0:T(8,128)(2,1)S(1)}, u32[]{:S(2)}, u32[]{:S(2)}) collective-permute-start(bf16[4,32,256]{2,1,0:T(8,128)(2,1)S(1)} %get-tuple-element.6), channel_id=1, source_target_pairs={{0,64},{64,128},{128,192},{192,0},{1,65},{65,129},{129,193},{193,1... | collective-permute-start | bytes 196616 | tf_op jit(solution)/shard_map/ppermute | solution.py:87
  157.4 5.2 %collective-permute-start.35 = (bf16[4,32,256]{2,1,0:T(8,128)(2,1)S(1)}, bf16[4,32,256]{2,1,0:T(8,128)(2,1)S(1)}, u32[]{:S(2)}, u32[]{:S(2)}) collective-permute-start(bf16[4,32,256]{2,1,0:T(8,128)(2,1)S(1)} %get-tuple-element.8), channel_id=1, source_target_pairs={{0,128},{64,192},{128,0},{192,64},{1,129},{65,193},{129,1},{193,65... | collective-permute-start | bytes 196616 | tf_op jit(solution)/shard_map/ppermute | solution.py:87
  174.4 4.1 %collective-permute-start.38 = (bf16[32,256]{1,0:T(8,128)(2,1)S(1)}, bf16[32,256]{1,0:T(8,128)(2,1)S(1)}, u32[]{:S(2)}, u32[]{:S(2)}) collective-permute-start(bf16[32,256]{1,0:T(8,128)(2,1)S(1)} %convolution_convert_fusion), channel_id=1, source_target_pairs={{0,2},{1,3},{2,0},{3,1},{4,6},{5,7},{6,4},{7,5},{8,10},{9,11},{10,... | collective-permute-start | bytes 49160 | tf_op jit(solution)/shard_map/ppermute | solution.py:92
  179.8 23.8 %collective-permute-start.40 = (bf16[2,32,256]{2,1,0:T(8,128)(2,1)S(1)}, bf16[2,32,256]{2,1,0:T(8,128)(2,1)S(1)}, u32[]{:S(2)}, u32[]{:S(2)}) collective-permute-start(bf16[2,32,256]{2,1,0:T(8,128)(2,1)S(1)} %pad_maximum_fusion.8), channel_id=1, source_target_pairs={{0,4},{4,0},{1,5},{5,1},{2,6},{6,2},{3,7},{7,3},{8,12},{12,8},{9,1... | collective-permute-start | bytes 98312 | tf_op jit(solution)/shard_map/ppermute | solution.py:16
  (14 other events, 83.8 us)
